TPU v7x, 1024 devices: a whole 8x8x8 slice. The times are simulated.
1024 devices in a mesh: group: 8 (over y), shard: 32 (over x, z_hi), mp: 4 (over z_lo, core).
Axes of the slice: x: 8, y: 8, z: 8 (z_hi: 4, z_lo: 2; z = z_hi * 2 + z_lo), core: 2. Of those that a mesh axis runs over, the one named last changes fastest.
Arguments:
- passage_states: bfloat16 [65536, 768], P(('group', 'shard', 'mp')), may hold values from -6 to 6
- query_emb: bfloat16 [8192, 768], P(('group', 'shard', 'mp')), may hold values from -82 to 82
- head_weight: bfloat16 [768, 768], replicated, may hold values from -0.21875 to 0.21875
- head_bias: float32 [768], replicated, may hold values from -4 to 4
- norm_gain: float32 [768], replicated, may hold values from 0.25 to 1.75
- candidate_ids: int32 [8192, 65], P(('group', 'shard', 'mp')), may hold values from 0 to 65535, as said below
Outputs:
- losses: float32 [8192], P(('group', 'shard', 'mp'))
- query_grad: float32 [8192, 768], P(('group', 'shard', 'mp'))
Inputs may be any that keep to these rules, and one draw needn't show every extreme that they name: `candidate_ids`: index row r belongs to owner ((r // 64) // 4) % 32. Among the 520 candidates of the queries of one device, exactly 40 lie in the rows of one owner drawn from the seed, and the rest are spread as evenly as possible over the other owners; rows within an owner are drawn evenly and may repeat.
All inputs are finite; a program needn't handle non-finite values.
Results may differ from a plain program's by a relative error of at most 0.014.
Values may be sent and summed in bfloat16 or wider, within the bound.
A program may use at most 32 MiB of HBM per device.

v0:
```python
import math

import jax
import jax.numpy as jnp
from jax import lax
from jax.sharding import PartitionSpec as P


def encode(states, weight, head_bias, gains):
    hidden = jnp.dot(states, weight, preferred_element_type=jnp.float32) + head_bias
    average = jnp.mean(hidden, axis=-1, keepdims=True)
    centred = hidden - average
    spread = jnp.mean(centred * centred, axis=-1, keepdims=True)
    return (centred * lax.rsqrt(spread + 1e-05) * gains).astype(jnp.bfloat16)


def local(passage_states, query_emb, head_weight, head_bias, norm_gain, candidate_ids):
    shards = lax.axis_size("shard")
    mp_parts = lax.axis_size("mp")
    rows_dev = passage_states.shape[0]
    width = passage_states.shape[1]
    qcount, cands = candidate_ids.shape
    slot_count = qcount * cands
    capacity = 5 * cands * qcount // (2 * shards)
    scaling = 1.0 / math.sqrt(width)
    fresh_rows = encode(passage_states, head_weight, head_bias, norm_gain)
    slab = lax.all_gather(fresh_rows, ("group", "mp"), axis=0, tiled=True)
    slab_rows = slab.shape[0]
    flat_ids = candidate_ids.reshape(slot_count)
    blocks = flat_ids // rows_dev
    within = flat_ids % rows_dev
    part_of = blocks % mp_parts
    owners = blocks // mp_parts % shards
    group_of = blocks // (mp_parts * shards)
    slab_index = (group_of * mp_parts + part_of) * rows_dev + within
    onehot = (owners[:, None] == jnp.arange(shards)[None, :]).astype(jnp.int32)
    earlier = jnp.cumsum(onehot, axis=0) - onehot
    places = jnp.sum(earlier * onehot, axis=1)
    slots = owners * capacity + places
    packed = jnp.arange(slot_count, dtype=jnp.int32) * slab_rows + slab_index
    request = (
        jnp.full((shards * capacity,), -1, jnp.int32)
        .at[slots]
        .set(packed)
        .reshape(shards, capacity)
    )
    incoming = lax.all_to_all(request, "shard", split_axis=0, concat_axis=0, tiled=True)
    filled = incoming >= 0
    inc_row = jnp.where(filled, incoming % slab_rows, 0)
    fetched = slab[inc_row]
    returned = lax.all_to_all(fetched, "shard", split_axis=0, concat_axis=0, tiled=True)
    picked = returned.reshape(shards * capacity, width)[slots].reshape(qcount, cands, width)
    scores = (
        jnp.einsum("qd,qcd->qc", query_emb, picked, preferred_element_type=jnp.float32) * scaling
    )
    highest = jnp.max(scores, axis=1, keepdims=True)
    weights = jnp.exp(scores - highest)
    totals = jnp.sum(weights, axis=1, keepdims=True)
    losses = highest[:, 0] + jnp.log(totals[:, 0]) - scores[:, 0]
    chances = weights / totals
    picked_wide = picked.astype(jnp.float32)
    mean_row = jnp.einsum("qc,qcd->qd", chances, picked_wide)
    gradient = (mean_row - picked_wide[:, 0]) * scaling
    return (losses, gradient)


def solution(mesh):
    in_specs = (
        P(("group", "shard", "mp"), None),
        P(("group", "shard", "mp"), None),
        P(),
        P(),
        P(),
        P(("group", "shard", "mp"), None),
    )
    out_specs = (P(("group", "shard", "mp")), P(("group", "shard", "mp"), None))
    return jax.shard_map(local, mesh=mesh, in_specs=in_specs, out_specs=out_specs, check_vma=False)
```

profile of v0, /device:TPU:6, one launch (start us, length us, event | category | flops | bytes accessed | tf_op | source)
XLA Modules:
  0.0 186.2 jit_solution(8277683232489747793)
XLA Ops:
  7.2 0.0 copy-start
  7.2 0.0 copy-start.1
  7.2 0.0 all-gather.2.cloned.1.call-start
  7.2 1.2 copy-done
  8.4 1.3 fusion.29
  9.8 0.2 multiply_reduce_fusion
  10.0 1.4 multiply_convert_fusion
  11.4 0.0 all-gather.2.cloned.1.call-update
  11.4 0.0 copy-done.1
  11.4 0.1 reshape.295
  11.5 0.1 reshape.296
  11.7 1.5 reduce-window.6
  13.1 0.3 slice_reduce_fusion
  13.4 0.1 bitcast_bitcast_fusion
  13.6 0.1 fusion.23
  13.6 4.1 %scatter_custom_fusion = s32[1280]{0:T(1024)S(1)} fusion(s32[520]{0:T(1024)S(1)} %fusion.23, s32[520]{0:T(1024)S(1)} %get-tuple-element.4, s32[]{:T(128)} %constant.95.clone.1), kind=kCustom, calls=%fused_computation.72 | custom fusion | bytes 5124 | tf_op jit(solution)/shard_map/scatter | solution.py:44
  17.7 0.1 all_to_all.11
  17.8 30.4 %all_to_all.17 = s32[32,1,40]{2,1,0:T(1,128)S(1)} all-to-all(s32[32,1,40]{2,1,0:T(1,128)S(1)} %all_to_all.11), channel_id=1, replica_groups=mesh['group'=8,'shard'=32,'mp'=4] {'shard'}, dimensions={0} | all-to-all | bytes 10240 | tf_op jit(solution)/shard_map/all_to_all | solution.py:47
  48.3 0.1 reshape.305
  48.4 45.8 %all-gather.2.cloned.1.call-done = bf16[2048,768]{1,0:T(8,128)(2,1)} async-done(((bf16[64,768]{1,0:T(8,128)(2,1)}), bf16[2048,768]{1,0:T(8,128)(2,1)}) %all-gather.2.cloned.1.call-update) | async-done | bytes 3145744 | tf_op jit(solution)/shard_map/all_gather | solution.py:27
  94.1 8.1 %gather_fusion = bf16[1280,768]{1,0:T(8,128)(2,1)} fusion(bf16[2048,768]{1,0:T(8,128)(2,1)} %all-gather.2.cloned.1.call-done, s32[2048]{0:T(1024)S(1)} %pad_clamp_fusion), kind=kCustom, calls=%fused_computation | custom fusion | bytes 3937280 | tf_op jit(solution)/shard_map/gather | solution.py:50
  102.2 13.2 %all-to-all-start.1 = ((bf16[32,40,768]{2,1,0:T(8,128)(2,1)}), bf16[32,40,768]{2,1,0:T(8,128)(2,1)S(1)}, u32[]{:S(2)}, u32[]{:S(2)}) async-start(bf16[32,40,768]{2,1,0:T(8,128)(2,1)} %bitcast.46), calls=%async_computation.1 | async-start | bytes 3932160 | tf_op jit(solution)/shard_map/all_to_all | solution.py:51
  115.4 57.2 %all-to-all-done.1 = bf16[32,40,768]{2,1,0:T(8,128)(2,1)S(1)} async-done(((bf16[32,40,768]{2,1,0:T(8,128)(2,1)}), bf16[32,40,768]{2,1,0:T(8,128)(2,1)S(1)}, u32[]{:S(2)}, u32[]{:S(2)}) %all-to-all-start.1) | async-done | bytes 1966112 | tf_op jit(solution)/shard_map/all_to_all | solution.py:51
  172.6 3.3 %gather_fusion.1 = bf16[520,768]{1,0:T(8,128)(2,1)} fusion(bf16[1280,768]{1,0:T(8,128)(2,1)S(1)} %bitcast.45, s32[1024]{0:T(1024)S(1)} %pad_clamp_fusion.1), kind=kCustom, calls=%fused_computation.1 | custom fusion | bytes 1599520 | tf_op jit(solution)/shard_map/gather | solution.py:52
  175.9 1.4 reshape.300
  177.3 0.0 copy-done.2
  177.3 0.3 fusion.4
  177.7 0.1 copy.12
  177.9 0.1 copy.13
  178.0 0.3 fusion.30
  178.2 0.5 fusion.27
  178.7 0.6 fusion.3
  (15 shorter events, 0.2 us)
Async XLA Ops:
  7.2 1.3 copy-start
  7.2 4.3 %copy-start.1 = (s32[8,65]{1,0:T(8,128)S(1)}, s32[8,65]{1,0:T(8,128)}, u32[]{:S(2)}) copy-start(s32[8,65]{1,0:T(8,128)} %param.11) | copy-start | bytes 6244
  7.2 87.0 %all-gather.2.cloned.1.call-start = ((), (), s32[]{:S(2)}) async-start(), calls=%async_computation.2 | async-start | bytes 3244032 | tf_op jit(solution)/shard_map/all_gather | solution.py:27
  102.2 70.4 %all-to-all-start.1 = ((bf16[32,40,768]{2,1,0:T(8,128)(2,1)}), bf16[32,40,768]{2,1,0:T(8,128)(2,1)S(1)}, u32[]{:S(2)}, u32[]{:S(2)}) async-start(bf16[32,40,768]{2,1,0:T(8,128)(2,1)} %bitcast.46), calls=%async_computation.1 | async-start | bytes 3932160 | tf_op jit(solution)/shard_map/all_to_all | solution.py:51
  172.6 4.7 %copy-start.2 = (bf16[8,768]{1,0:T(8,128)(2,1)S(1)}, bf16[8,768]{1,0:T(8,128)(2,1)}, u32[]{:S(2)}) copy-start(bf16[8,768]{1,0:T(8,128)(2,1)} %param.7) | copy-start | bytes 36868
Sparse Core Ops, SparseCore 0:
  11.6 82.5 all-gather.1
where the time goes:
time: 187 us; the launch traced here: 186 us
  waiting for transfers between devices  103 us (55%)
  blocking collectives  30.4 us (16%)
  local copies, waits for them, and re-layouts  18.9 us (10%)
  between operations  14.2 us (8%)
  starting transfers between devices  13.2 us (7%)
  other arithmetic  4.6 us (2%)
  matrix products  1.93 us (1%)
    all_to_all x1, waiting for transfers between devices, local(): lax.all_to_all(fetched, 'shard', split_axis=0, concat_axis=0, tiled=True)  57.2 us
    all_gather x1, waiting for transfers between devices, local(): slab = lax.all_gather(fresh_rows, ('group', 'mp'), axis=0, tiled=True)  45.8 us
    all_to_all x1, blocking collectives, local(): lax.all_to_all(request, 'shard', split_axis=0, concat_axis=0, tiled=True)  30.4 us
    all_to_all x1, starting transfers between devices, local(): lax.all_to_all(fetched, 'shard', split_axis=0, concat_axis=0, tiled=True)  13.2 us
    gather x1, local copies, waits for them, and re-layouts, local(): fetched = slab[inc_row]  8.09 us
    scatter x1, local copies, waits for them, and re-layouts, local(): request = jnp.full((shards * capacity,), -1, jnp.int32).at[slots].set(pac...  4.1 us
  transfers between devices with their start and end apart: 2, of which 2 were waited for; matrix products, arithmetic and copies ran while one was open for 3% of the time, Pallas kernels for 0%

commit v1 on v0

v1 whole, which is shorter than its diff:
```python
import functools
import math

import jax
import jax.numpy as jnp
from jax import lax
from jax.experimental import pallas as pl
from jax.experimental.pallas import tpu as pltpu
from jax.sharding import PartitionSpec as P

MESH = pl.DeviceIdType.MESH
NT = (((1,), (1,)), ((), ()))
LOW = -1e30
REACH = ((4, 3), (3, 4), (4, 3))


def kernel(
    rings, owners, rows, queries,
    states, query, ids, bias, gain, w_hbm,
    stat_out, grad_out,
    w, slab, qbuf, qmat, idbuf, cnt, score, prob, part, parts, stat, stats, back,
    w_sem, ys, yr, zs, zr, cs, cr, qs, qr, ds, dr, ts, tr, ps, pr,
):
    width = states.shape[1]
    half_width = width // 2
    half = rows // 2
    span = 4 * rows
    scaling = 1.0 / math.sqrt(width)
    g, s, mp = lax.axis_index("group"), lax.axis_index("shard"), lax.axis_index("mp")
    right = {"group": lax.rem(g + 1, rings)}
    left = {"group": lax.rem(g + rings - 1, rings)}
    across = lax.rem(mp + 2, 4)
    twin = mp + 1 - 2 * lax.rem(mp, 2)
    twin_across = lax.rem(twin + 2, 4)

    load_w = pltpu.make_async_copy(w_hbm, w, w_sem)
    load_w.start()
    barrier = pltpu.get_barrier_semaphore()
    for other in (right, left, {"mp": across}, {"mp": twin}):
        pl.semaphore_signal(barrier, inc=1, device_id=other, device_id_type=MESH)

    def greet(k, carry):
        other = {"shard": lax.rem(s + k, owners)}
        pl.semaphore_signal(barrier, inc=1, device_id=other, device_id_type=MESH)
        return carry

    lax.fori_loop(1, owners, greet, 0)

    own = pl.multiple_of(g * span + mp * rows, rows)
    load_w.wait()
    hidden = jnp.dot(states[...], w[...], preferred_element_type=jnp.float32) + bias[...]
    centred = hidden - jnp.mean(hidden, axis=-1, keepdims=True)
    spread = jnp.mean(centred * centred, axis=-1, keepdims=True)
    slab[pl.ds(own, rows), :] = (centred * lax.rsqrt(spread + 1e-05) * gain[...]).astype(jnp.bfloat16)
    q_own = pl.ds(pl.multiple_of(s * 2 * queries, 2 * queries), 2 * queries)
    d_own = pl.ds(pl.multiple_of(s * 8, 8), 8)
    qbuf[q_own, :] = query[...]
    idbuf[d_own, :] = ids[...]
    pl.semaphore_wait(barrier, owners + 3)

    def send(src, dst, send_sem, recv_sem, other):
        return pltpu.make_async_remote_copy(
            src_ref=src, dst_ref=dst, send_sem=send_sem, recv_sem=recv_sem,
            device_id=other, device_id_type=MESH,
        )

    def chunk(ring, lane, part_of):
        return slab.at[pl.ds(pl.multiple_of(ring * span + lane * rows + part_of * half, half), half), :]

    def origin(way, k):
        return lax.rem(g + (rings - k if way == 0 else k), rings)

    def y_copy(stream, way, k, ring):
        c = chunk(ring, across if stream == 2 else mp, 0 if stream == 0 else 1)
        sem = (stream * 2 + way) * 4 + k - 1
        return send(c, c, ys.at[sem], yr.at[sem], right if way == 0 else left)

    def z_copy(ring, lane, part_of):
        c = chunk(ring, lane, part_of)
        sem = ring if part_of == 0 else rings
        return send(c, c, zs.at[sem], zr.at[sem], {"mp": across})

    def c_copy(ring, lane, part_of):
        c = chunk(ring, lane, part_of)
        sem = ring * 4 + lane // 2 * 2 + part_of
        return send(c, c, cs.at[sem], cr.at[sem], {"mp": twin})

    z_copy(g, mp, 1).start()
    for stream in (1, 0):
        for way in (0, 1):
            y_copy(stream, way, 1, g).start()
    z_copy(g, mp, 0).start()
    c_copy(g, mp, 0).start()
    c_copy(g, mp, 1).start()

    def q_copy(p, at):
        there = pl.ds(pl.multiple_of(at * 2 * queries, 2 * queries), 2 * queries)
        return send(query, qbuf.at[there, :], qs.at[p], qr.at[at], {"shard": p})

    def d_copy(p, at):
        there = pl.ds(pl.multiple_of(at * 8, 8), 8)
        return send(ids, idbuf.at[there, :], ds.at[p], dr.at[at], {"shard": p})

    def share(k, carry):
        p = lax.rem(s + k, owners)
        d_copy(p, s).start()
        q_copy(p, s).start()
        return carry

    lax.fori_loop(1, owners, share, 0)

    z_copy(g, across, 1).wait_recv()
    for way in (0, 1):
        y_copy(2, way, 1, g).start()
    c_copy(g, across, 1).start()
    z_copy(g, across, 0).wait_recv()
    c_copy(g, across, 0).start()

    def y_step(k):
        for stream in (2, 1, 0):
            for way in (0, 1):
                if k > REACH[stream][way]:
                    continue
                ring = origin(way, k)
                y_copy(stream, way, k, ring).wait_recv()
                if k < REACH[stream][way]:
                    y_copy(stream, way, k + 1, ring).start()
                if stream == 0:
                    z_copy(ring, mp, 0).start()
                c_copy(ring, across if stream == 2 else mp, 0 if stream == 0 else 1).start()

    def z_step(k):
        for way in (0, 1):
            if k <= REACH[0][way]:
                ring = origin(way, k)
                z_copy(ring, across, 0).wait_recv()
                c_copy(ring, across, 0).start()

    def await_ids(k, carry):
        p = lax.rem(s + k, owners)
        d_copy(p, p).wait_recv()
        return carry

    def await_queries(k, carry):
        p = lax.rem(s + k, owners)
        q_copy(p, p).wait_recv()
        return carry

    def multiplicity(j, carry):
        packed = idbuf[pl.ds(pl.multiple_of(j * 8, 8), 8), :]
        sub = lax.broadcasted_iota(jnp.int32, (128, 128), 0)
        total = jnp.zeros((128, 128), jnp.float32)
        for t in range(5):
            row = packed[t : t + 1, :]
            key = ((row & 0xFFFFF) >> 7) - s * 128
            value = jnp.where((row >> 20) > 0, 129.0, 1.0)
            left_hot = jnp.where(sub == key, value, 0.0).astype(jnp.bfloat16)
            right_hot = jnp.where(sub == (row & 127), 1.0, 0.0).astype(jnp.bfloat16)
            total += lax.dot_general(left_hot, right_hot, NT, preferred_element_type=jnp.float32)
        for hi in range(16):
            cnt[pl.ds(pl.multiple_of(j * 8, 8), 8), hi * 128 : hi * 128 + 128] = total[hi * 8 : hi * 8 + 8, :]
        return carry

    def scores(ring):
        at = pl.ds(pl.multiple_of(ring * span, span), span)
        score[:, at] = lax.dot_general(qmat[...], slab[at, :], NT, preferred_element_type=jnp.float32) * scaling

    def block(k):
        for ring in {0: (g,), 4: (origin(1, 4),)}.get(k, (origin(0, k), origin(1, k))):
            for lane in (twin, twin_across):
                for part_of in (0, 1):
                    c_copy(ring, lane, part_of).wait_recv()
            scores(ring)

    lax.fori_loop(1, owners, await_ids, 0)
    y_step(1)
    lax.fori_loop(0, owners // 2, multiplicity, 0)
    y_step(2)
    z_step(1)
    lax.fori_loop(owners // 2, owners, multiplicity, 0)
    y_step(3)
    z_step(2)
    lax.fori_loop(1, owners, await_queries, 0)
    wide = qbuf[...].astype(jnp.float32).reshape(owners, 2, queries, half_width)
    qmat[:, :half_width] = wide[:, 0].reshape(owners * queries, half_width).astype(jnp.bfloat16)
    qmat[:, half_width:] = wide[:, 1].reshape(owners * queries, half_width).astype(jnp.bfloat16)
    block(0)
    block(1)
    y_step(4)
    z_step(3)
    block(2)
    z_step(4)
    block(3)
    block(4)

    def softmax(j, carry):
        at = pl.ds(pl.multiple_of(j * 16, 16), 16)
        c = cnt[at, :]
        x = score[at, :]
        positive = c >= 128.0
        times = jnp.where(positive, c - 128.0, c)
        x_in = jnp.where(times > 0.0, x, LOW)
        top = jnp.max(x_in, axis=1, keepdims=True)
        e = times * jnp.exp(x_in - top)
        total = jnp.sum(e, axis=1, keepdims=True)
        first = jnp.sum(jnp.where(positive, x, 0.0), axis=1, keepdims=True)
        score[at, :] = e
        lane = lax.broadcasted_iota(jnp.int32, (16, 128), 1)
        stat[at, :] = jnp.where(lane == 0, top, jnp.where(lane == 1, total, jnp.where(lane == 2, first, 0.0)))
        return carry

    lax.fori_loop(0, owners * queries // 16, softmax, 0)
    mine = jnp.transpose(stat[...])[:8, :]
    stats[d_own, :] = mine

    def t_copy(p, at):
        there = stats.at[pl.ds(pl.multiple_of(at * 8, 8), 8), :]
        return send(there, there, ts.at[p], tr.at[at], {"shard": p})

    def tell(k, carry):
        t_copy(lax.rem(s + k, owners), s).start()
        return carry

    def told(k, carry):
        p = lax.rem(s + k, owners)
        t_copy(p, p).wait_recv()
        return carry

    lax.fori_loop(1, owners, tell, 0)
    lax.fori_loop(1, owners, told, 0)
    every = stats[...].reshape(owners, 8, owners * queries)
    top = jnp.max(every, axis=0)[0:1, :]
    share_of = jnp.exp(every[:, 0:1, :] - top.reshape(1, 1, owners * queries))
    total = jnp.sum(every * share_of, axis=0)[1:2, :]
    first = jnp.sum(every, axis=0)[2:3, :]
    factor = jnp.exp(mine[0:1, :] - top) / total
    loss = top + jnp.log(total) - first
    line = lax.broadcasted_iota(jnp.int32, (128, owners * queries), 0)
    back[...] = jnp.transpose(jnp.where(line == 0, factor, jnp.where(line == 1, loss, 0.0)))
    stat_out[...] = back[d_own, :]

    def chances(j, carry):
        at = pl.ds(pl.multiple_of(j * 16, 16), 16)
        positive = jnp.where(cnt[at, :] >= 128.0, 1.0, 0.0)
        prob[at, :] = (score[at, :] * back[at, 0:1] - positive).astype(jnp.bfloat16)
        return carry

    lax.fori_loop(0, owners * queries // 16, chances, 0)

    def p_copy(p, frm, at):
        src = part.at[pl.ds(pl.multiple_of(frm * 2 * queries, 2 * queries), 2 * queries), :]
        there = parts.at[pl.ds(pl.multiple_of(at * 2 * queries, 2 * queries), 2 * queries), :]
        return send(src, there, ps.at[p], pr.at[at], {"shard": p})

    batch = owners // 4

    def gradients(i, carry):
        b = lax.rem(s // batch + i, 4)
        take = pl.ds(pl.multiple_of(b * batch * queries, batch * queries), batch * queries)
        grad = jnp.dot(prob[take, :], slab[...], preferred_element_type=jnp.float32) * scaling
        lo = grad[:, :half_width].reshape(batch, queries, half_width)
        hi = grad[:, half_width:].reshape(batch, queries, half_width)
        both = jnp.concatenate([lo, hi], axis=1).reshape(batch * 2 * queries, half_width)
        put = pl.ds(pl.multiple_of(b * batch * 2 * queries, batch * 2 * queries), batch * 2 * queries)
        part[put, :] = both.astype(jnp.bfloat16)

        def give(k, inner):
            p = b * batch + lax.rem(s + k, batch)

            @pl.when(p != s)
            def _():
                p_copy(p, p, s).start()

            return inner

        lax.fori_loop(0, batch, give, 0)
        return carry

    lax.fori_loop(0, 4, gradients, 0)
    parts[q_own, :] = part[q_own, :]

    def taken(k, carry):
        p = lax.rem(s + k, owners)
        p_copy(p, p, p).wait_recv()
        return carry

    lax.fori_loop(1, owners, taken, 0)
    summed = jnp.sum(parts[...].astype(jnp.float32).reshape(owners, 2 * queries, half_width), axis=0)
    grad_out[:, :half_width] = summed[:queries, :]
    grad_out[:, half_width:] = summed[queries:, :]

    def sent(k, carry):
        p = lax.rem(s + k, owners)
        q_copy(p, s).wait_send()
        d_copy(p, s).wait_send()
        t_copy(p, s).wait_send()
        p_copy(p, p, s).wait_send()
        return carry

    lax.fori_loop(1, owners, sent, 0)
    for stream in range(3):
        for way in (0, 1):
            for k in range(1, REACH[stream][way] + 1):
                y_copy(stream, way, k, origin(way, k - 1)).wait_send()

    def sent_across(ring, carry):
        z_copy(ring, mp, 0).wait_send()
        for lane in (mp, across):
            for part_of in (0, 1):
                c_copy(ring, lane, part_of).wait_send()
        return carry

    lax.fori_loop(0, rings, sent_across, 0)
    z_copy(g, mp, 1).wait_send()


def local(passage_states, query_emb, head_weight, head_bias, norm_gain, candidate_ids):
    rings, owners, parts = lax.axis_size("group"), lax.axis_size("shard"), lax.axis_size("mp")
    rows, width = passage_states.shape
    queries, cands = candidate_ids.shape
    span = parts * rows
    slab_rows = rings * span
    all_queries = owners * queries

    owner = candidate_ids // span % owners
    slab_index = candidate_ids // (span * owners) * span + candidate_ids % span
    line = lax.broadcasted_iota(jnp.int32, candidate_ids.shape, 0)
    column = lax.broadcasted_iota(jnp.int32, candidate_ids.shape, 1)
    key = slab_index // 128 * queries + line
    packed = (column == 0).astype(jnp.int32) * 2**20 + owner * 2**14 + key * 128 + slab_index % 128
    packed = jnp.pad(packed.reshape(-1), (0, 1024 - queries * cands), constant_values=63 * 2**14).reshape(8, 128)
    query = query_emb.reshape(queries, 2, width // 2).transpose(1, 0, 2).reshape(2 * queries, width // 2)

    vmem = pl.BlockSpec(memory_space=pltpu.VMEM)
    dma = pltpu.SemaphoreType.DMA
    bf16, f32 = jnp.bfloat16, jnp.float32
    stat, grad = pl.pallas_call(
        functools.partial(kernel, rings, owners, rows, queries),
        out_shape=(jax.ShapeDtypeStruct((queries, 128), f32), jax.ShapeDtypeStruct((queries, width), f32)),
        in_specs=[vmem] * 5 + [pl.BlockSpec(memory_space=pl.ANY)],
        out_specs=(vmem, vmem),
        scratch_shapes=[
            pltpu.VMEM((width, width), bf16),
            pltpu.VMEM((slab_rows, width), bf16),
            pltpu.VMEM((2 * all_queries, width // 2), bf16),
            pltpu.VMEM((all_queries, width), bf16),
            pltpu.VMEM((owners * 8, 128), jnp.int32),
            pltpu.VMEM((all_queries, slab_rows), f32),
            pltpu.VMEM((all_queries, slab_rows), f32),
            pltpu.VMEM((all_queries, slab_rows), bf16),
            pltpu.VMEM((2 * all_queries, width // 2), bf16),
            pltpu.VMEM((2 * all_queries, width // 2), bf16),
            pltpu.VMEM((all_queries, 128), f32),
            pltpu.VMEM((owners * 8, all_queries), f32),
            pltpu.VMEM((all_queries, 128), f32),
            dma,
            dma((24,)), dma((24,)),
            dma((rings + 1,)), dma((rings + 1,)),
            dma((rings * 4,)), dma((rings * 4,)),
            dma((owners,)), dma((owners,)),
            dma((owners,)), dma((owners,)),
            dma((owners,)), dma((owners,)),
            dma((owners,)), dma((owners,)),
        ],
        compiler_params=pltpu.CompilerParams(
            collective_id=0, has_side_effects=True, vmem_limit_bytes=40 * 2**20
        ),
    )(
        passage_states, query, packed, head_bias.reshape(1, width), norm_gain.reshape(1, width), head_weight,
    )
    return stat[:, 1], grad


def solution(mesh):
    split = P(("group", "shard", "mp"), None)
    in_specs = (split, split, P(), P(), P(), split)
    out_specs = (P(("group", "shard", "mp")), split)
    return jax.shard_map(local, mesh=mesh, in_specs=in_specs, out_specs=out_specs, check_vma=False)
```

time: 187 us -> 101 us (0.54)
  the two profiles are of different devices: /device:TPU:6 before, /device:TPU:1 now
where the time goes in v1:
time: 101 us
  Pallas kernels  93.6 us (93%)
  local copies, waits for them, and re-layouts  5.63 us (6%)
    pallas_call x1, Pallas kernels, local(): pl.pallas_call(functools.partial(kernel, rings, owners, rows, queries), o...  93.6 us
    unnamed x7, local copies, waits for them, and re-layouts  3.47 us

profile of v1, /device:TPU:1, one launch (start us, length us, event | category | flops | bytes accessed | tf_op | source)
XLA Modules:
  0.0 100.6 jit_solution(17267939032621545415)
XLA Ops:
  0.6 0.7 reshape.26.bias
  1.3 0.7 reshape.27.gain
  2.0 0.7 fusion.4
  2.7 0.1 reshape.24
  2.8 0.0 copy-start
  2.8 1.3 %copy-done = bf16[768,768]{1,0:T(8,128)(2,1)S(1)} copy-done((bf16[768,768]{1,0:T(8,128)(2,1)S(1)}, bf16[768,768]{1,0:T(8,128)(2,1)}, u32[]{:S(2)}) %copy-start) | copy-done | bytes 1179672
  4.1 0.0 copy-start.1
  4.1 0.9 copy-done.1
  5.0 0.0 copy-start.2
  5.0 0.7 copy-done.2
  5.7 93.6 %shard_map.77 = (f32[8,128]{1,0:T(8,128)S(1)}, f32[8,768]{1,0:T(8,128)S(1)}) custom-call(bf16[64,768]{1,0:T(8,128)(2,1)S(1)} %copy-done.1, bf16[16,384]{1,0:T(8,128)(2,1)S(1)} %bitcast.7, s32[8,128]{1,0:T(8,128)S(1)} %pad_bitcast_fusion.ids, f32[1,768]{1,0:T(1,128)S(1)} %reshape.26.bias, f32[1,768]{1,0:T(1,128)S(1)} %reshape.27.gain, ...), custom_call_target="tpu_custom_call" | custom-call | tf_op jit(solution)/shard_map/pallas_call | solution.py:337
  99.3 0.7 slice_reduce_fusion
  100.0 0.6 copy.9
  (2 shorter events, 0.0 us)
Async XLA Ops:
  2.8 1.3 %copy-start = (bf16[768,768]{1,0:T(8,128)(2,1)S(1)}, bf16[768,768]{1,0:T(8,128)(2,1)}, u32[]{:S(2)}) copy-start(bf16[768,768]{1,0:T(8,128)(2,1)} %w_hbm.1) | copy-start | bytes 3538948
  4.1 0.9 copy-start.1
  5.0 0.7 copy-start.2

commit v2 on v0

v2 whole, which is shorter than its diff:
```python
import functools
import math

import jax
import jax.numpy as jnp
from jax import lax
from jax.experimental import pallas as pl
from jax.experimental.pallas import tpu as pltpu
from jax.sharding import PartitionSpec as P

MESH = pl.DeviceIdType.MESH
NT = (((1,), (1,)), ((), ()))
LOW = -1e30
F32, BF16 = jnp.float32, jnp.bfloat16


def kernel(
    owners, rows, queries, cands,
    states_in, query_in, w_in, bias_in, gain_in, ids_in,
    loss_out, grad_out,
    states, query, w, bias, gain, raw_ids, query_half, ids,
    slab, qbuf, qmat, idbuf, cnt, score, prob, first, part, parts, stat, stats,
    load_sems, us, ur, ns, nr, vs, vr, cs, cr, qs, qr, ds, dr, ts, tr, ps, pr,
):
    width = w.shape[0]
    half_width = width // 2
    half = rows // 2
    span = 4 * rows
    every = owners * queries
    two = 2 * queries
    scaling = 1.0 / math.sqrt(width)
    y, s, mp = lax.axis_index("group"), lax.axis_index("shard"), lax.axis_index("mp")
    x, z = s // 4, lax.rem(s, 4) * 2 + mp // 2
    core, y_lo = lax.rem(mp, 2), lax.rem(y, 2)
    me = x * 4 + y // 2
    lane = y_lo * 2 + core
    lane_across = lax.rem(lane + 2, 4)
    lane_twin = lane + 1 - 2 * core
    lane_twin_across = lax.rem(lane_twin + 2, 4)

    def at_z(level):
        return {"shard": x * 4 + level // 2, "mp": lax.rem(level, 2) * 2 + core}

    above, below = at_z(lax.rem(z + 1, 8)), at_z(lax.rem(z + 7, 8))
    across = {"group": y + 1 - 2 * y_lo}
    twin = {"mp": mp + 1 - 2 * core}

    def peer(p):
        return {"group": lax.rem(p, 4) * 2 + y_lo, "shard": p // 4 * 4 + s - x * 4}

    def other(k):
        return lax.rem(me + k, owners)

    loads = [
        pltpu.make_async_copy(src, dst, load_sems.at[i])
        for i, (src, dst) in enumerate(
            ((w_in, w), (states_in, states), (bias_in, bias), (gain_in, gain), (query_in, query), (ids_in, raw_ids))
        )
    ]
    for load in loads:
        load.start()

    barrier = pltpu.get_barrier_semaphore()

    def greet(device):
        pl.semaphore_signal(barrier, inc=1, device_id=device, device_id_type=MESH)

    greet(below)

    @pl.when(z < 7)
    def _():
        greet(above)

    greet(across)
    greet(twin)

    def greet_peer(k, carry):
        greet(peer(other(k)))
        return carry

    lax.fori_loop(1, owners, greet_peer, 0)

    for load in loads:
        load.wait()
    hidden = jnp.dot(states[...], w[...], preferred_element_type=F32) + bias[...].reshape(1, width)
    centred = hidden - jnp.mean(hidden, axis=-1, keepdims=True)
    spread = jnp.mean(centred * centred, axis=-1, keepdims=True)
    normal = centred * lax.rsqrt(spread + 1e-05) * gain[...].reshape(1, width)
    slab[pl.ds(pl.multiple_of(z * span + lane * rows, rows), rows), :] = normal.astype(BF16)
    pl.semaphore_wait(barrier, owners + 2 + (z > 0).astype(jnp.int32))

    def send(src, dst, send_sem, recv_sem, device):
        return pltpu.make_async_remote_copy(
            src_ref=src, dst_ref=dst, send_sem=send_sem, recv_sem=recv_sem, device_id=device, device_id_type=MESH,
        )

    def chunk(level, which, h):
        return slab.at[pl.ds(pl.multiple_of(level * span + which * rows + h * half, half), half), :]

    def up(level, h):
        c, sem = chunk(level, lane, h), level * 2 + h
        return send(c, c, us.at[sem], ur.at[sem], above)

    def down(level, h):
        c, sem = chunk(level, lane, h), level * 2 + h
        return send(c, c, ns.at[sem], nr.at[sem], below)

    def over(level, h, which):
        c, sem = chunk(level, which, h), level * 2 + h
        return send(c, c, vs.at[sem], vr.at[sem], across)

    def to_twin(level, h, which):
        c, sem = chunk(level, which, h), level * 4 + which // 2 * 2 + h
        return send(c, c, cs.at[sem], cr.at[sem], twin)

    def reach_up(level):
        return jnp.where(level >= 6, 3, 7 - level)

    def reach_down(level):
        return jnp.where(level >= 6, 4, level)

    for h in (0, 1):
        up(z, h).start()

        @pl.when(z > 0)
        def _(h=h):
            down(z, h).start()

    for h in (0, 1):
        over(z, h, lane).start()
        to_twin(z, h, lane).start()

    wide = query[...].astype(F32)
    query_half[...] = jnp.concatenate([wide[:, :half_width], wide[:, half_width:]], axis=0).astype(BF16)
    raw = raw_ids[...]
    line = lax.broadcasted_iota(jnp.int32, raw.shape, 0)
    column = lax.broadcasted_iota(jnp.int32, raw.shape, 1)
    ring_of = (raw >> 8) & 31
    y_of = raw >> 13
    z_of = (ring_of & 3) * 2 + ((raw >> 7) & 1)
    owner_of = (ring_of >> 2) * 4 + (y_of >> 1)
    key_of = (z_of * 2 + (y_of & 1)) * queries + line
    packed = jnp.where(column == 0, 2**20, 0) + owner_of * 2**14 + key_of * 2**7 + (raw & 127)
    ids[...] = jnp.full(ids.shape, 63 * 2**14, jnp.int32)
    ids[:, :cands] = packed

    def q_at(p):
        return pl.ds(pl.multiple_of(p * two, two), two)

    def d_at(p):
        return pl.ds(pl.multiple_of(p * 8, 8), 8)

    def q_copy(p, at):
        return send(query_half, qbuf.at[q_at(at), :], qs.at[p], qr.at[at], peer(p))

    def d_copy(p, at):
        return send(ids, idbuf.at[d_at(at), :], ds.at[p], dr.at[at], peer(p))

    def share(k, carry):
        d_copy(other(k), me).start()
        q_copy(other(k), me).start()
        return carry

    lax.fori_loop(1, owners, share, 0)
    qbuf[q_at(me), :] = query_half[...]
    idbuf[d_at(me), :] = ids[...]

    def await_share(k, carry):
        p = other(k)
        d_copy(p, p).wait_recv()
        q_copy(p, p).wait_recv()
        return carry

    def multiplicity(j, carry):
        block = idbuf[d_at(j), :]
        sub = lax.broadcasted_iota(jnp.int32, (128, 128), 0)
        total = jnp.zeros((128, 128), F32)
        for t in range(queries):
            row = block[t : t + 1, :]
            key = ((row & 0xFFFFF) >> 7) - me * 128
            value = jnp.where((row >> 20) > 0, 129.0, 1.0)
            left_hot = jnp.where(sub == key, value, 0.0).astype(BF16)
            right_hot = jnp.where(sub == (row & 127), 1.0, 0.0).astype(BF16)
            total += lax.dot_general(left_hot, right_hot, NT, preferred_element_type=F32)
        for hi in range(16):
            cnt[d_at(j), hi * 128 : hi * 128 + 128] = total[hi * 8 : hi * 8 + 8, :]
        return carry

    def rise(k, when):
        level = lax.rem(z - k + 16, 8)
        return when, level, k + 1 <= reach_up(level), up

    def fall(k):
        level = lax.rem(z + k, 8)
        return jnp.logical_and(z + k <= 7, k <= reach_down(level)), level, k + 1 <= reach_down(level), down

    arrivals = []
    for k in range(1, 8):
        arrivals.append(rise(k, z >= k))
        if k <= 5:
            arrivals.append(fall(k))
        if k == 3:
            arrivals.append(rise(z + 1, z <= 2))
        if k == 4:
            arrivals.append(rise(z + 2, z <= 1))

    def arrive(event):
        when, level, goes_on, way = event

        @pl.when(when)
        def _():
            for h in (0, 1):
                way(level, h).wait_recv()

                @pl.when(goes_on)
                def _(h=h):
                    way(level, h).start()

                over(level, h, lane).start()
                to_twin(level, h, lane).start()

    def pass_on(level):
        for h in (0, 1):
            over(level, h, lane_across).wait_recv()
            to_twin(level, h, lane_across).start()

    def use(level):
        for which in (lane_twin, lane_twin_across):
            for h in (0, 1):
                to_twin(level, h, which).wait_recv()
        at = pl.ds(pl.multiple_of(level * span, span), span)
        score[:, at] = lax.dot_general(qmat[...], slab[at, :], NT, preferred_element_type=F32) * scaling

    def later(event, do):
        @pl.when(event[0])
        def _():
            do(event[1])

    pass_on(z)
    for event in arrivals[:4]:
        arrive(event)
    for event in arrivals[:3]:
        later(event, pass_on)
    lax.fori_loop(1, owners, await_share, 0)
    lax.fori_loop(0, owners, multiplicity, 0)
    halves = qbuf[...].astype(F32).reshape(owners, 2, queries, half_width)
    qmat[:, :half_width] = halves[:, 0].reshape(every, half_width).astype(BF16)
    qmat[:, half_width:] = halves[:, 1].reshape(every, half_width).astype(BF16)
    use(z)
    later(arrivals[0], use)
    later(arrivals[1], use)
    for i in range(4, len(arrivals)):
        arrive(arrivals[i])
        later(arrivals[i - 1], pass_on)
        later(arrivals[i - 2], use)
    later(arrivals[-1], pass_on)
    later(arrivals[-2], use)
    later(arrivals[-1], use)

    def softmax(i, carry):
        at = pl.ds(pl.multiple_of(i * 16, 16), 16)
        c = cnt[at, :]
        v = score[at, :]
        positive = c >= 128.0
        times = jnp.where(positive, c - 128.0, c)
        inside = jnp.where(times > 0.0, v, LOW)
        top = jnp.max(inside, axis=1, keepdims=True)
        e = times * jnp.exp(inside - top)
        total = jnp.sum(e, axis=1, keepdims=True)
        named = jnp.sum(jnp.where(positive, v, 0.0), axis=1, keepdims=True)
        prob[at, :] = e.astype(BF16)
        first[at, :] = jnp.where(positive, 1.0, 0.0).astype(BF16)
        spot = lax.broadcasted_iota(jnp.int32, (16, 128), 1) - 4 * (lax.broadcasted_iota(jnp.int32, (16, 128), 0) & 7)
        tile = jnp.where(spot == 0, top, jnp.where(spot == 1, total, jnp.where(spot == 2, named, 0.0)))
        stat[pl.ds(i * 2, 2), :, :] = jnp.sum(tile.reshape(2, 8, 128), axis=1, keepdims=True)
        return carry

    lax.fori_loop(0, every // 16, softmax, 0)

    def t_copy(p, at):
        return send(stat.at[p], stats.at[at], ts.at[p], tr.at[at], peer(p))

    def tell(k, carry):
        t_copy(other(k), me).start()
        return carry

    lax.fori_loop(1, owners, tell, 0)
    stats[pl.ds(me, 1), :, :] = stat[pl.ds(me, 1), :, :]

    def p_at(p):
        return pl.ds(pl.multiple_of(p * 2 * two, 2 * two), 2 * two)

    def p_copy(p, frm, at):
        return send(part.at[p_at(frm), :], parts.at[p_at(at), :], ps.at[p], pr.at[at], peer(p))

    batch = owners // 4

    def partials(i, carry):
        b = lax.rem(me // batch + 2 + i, 4)
        take = pl.ds(pl.multiple_of(b * batch * queries, batch * queries), batch * queries)
        pieces = []
        for weights in (prob, first):
            sums = jnp.dot(weights[take, :], slab[...], preferred_element_type=F32)
            pieces.append(sums[:, :half_width].reshape(batch, queries, half_width))
            pieces.append(sums[:, half_width:].reshape(batch, queries, half_width))
        put = pl.ds(pl.multiple_of(b * batch * 2 * two, batch * 2 * two), batch * 2 * two)
        part[put, :] = jnp.concatenate(pieces, axis=1).reshape(batch * 2 * two, half_width).astype(BF16)

        def give(k, inner):
            p = b * batch + lax.rem(me + k, batch)

            @pl.when(p != me)
            def _():
                p_copy(p, p, me).start()

            return inner

        lax.fori_loop(0, batch, give, 0)
        return carry

    lax.fori_loop(0, 4, partials, 0)
    parts[p_at(me), :] = part[p_at(me), :]

    def told(k, carry):
        t_copy(other(k), other(k)).wait_recv()
        return carry

    lax.fori_loop(1, owners, told, 0)
    told_all = stats[...].reshape(owners, 128)
    top = jnp.max(told_all, axis=0, keepdims=True)
    fade = jnp.exp(jnp.minimum(told_all - top, 0.0))
    total = jnp.sum(pltpu.roll(told_all, 127, 1) * fade, axis=0, keepdims=True)
    named = jnp.sum(pltpu.roll(told_all, 126, 1), axis=0, keepdims=True)
    own_spot = lax.broadcasted_iota(jnp.int32, (1, queries, 128), 2) == 4 * lax.broadcasted_iota(
        jnp.int32, (1, queries, 128), 1
    )

    def upright(flat):
        return jnp.sum(jnp.where(own_spot, flat.reshape(-1, 1, 128), 0.0), axis=2, keepdims=True)

    factor = upright(fade / total)
    loss_out[...] = jnp.broadcast_to(upright(top + jnp.log(total) - named)[0], (queries, 128))

    def taken(k, carry):
        p = other(k)
        p_copy(p, p, p).wait_recv()
        return carry

    lax.fori_loop(1, owners, taken, 0)
    got = parts[...].astype(F32).reshape(owners, 4, queries, half_width)
    for i in (0, 1):
        mean_row = jnp.sum(got[:, i] * factor, axis=0)
        grad_out[:, i * half_width : (i + 1) * half_width] = (mean_row - jnp.sum(got[:, 2 + i], axis=0)) * scaling

    def sent(k, carry):
        p = other(k)
        q_copy(p, me).wait_send()
        d_copy(p, me).wait_send()
        t_copy(p, me).wait_send()
        p_copy(p, p, me).wait_send()
        return carry

    lax.fori_loop(1, owners, sent, 0)

    def sent_rows(level, carry):
        risen, fallen = lax.rem(z - level + 8, 8), level - z

        @pl.when(risen + 1 <= reach_up(level))
        def _():
            for h in (0, 1):
                up(level, h).wait_send()

        @pl.when(jnp.logical_and(fallen >= 0, fallen + 1 <= reach_down(level)))
        def _():
            for h in (0, 1):
                down(level, h).wait_send()

        for h in (0, 1):
            over(level, h, lane).wait_send()
            to_twin(level, h, lane).wait_send()
            to_twin(level, h, lane_across).wait_send()
        return carry

    lax.fori_loop(0, 8, sent_rows, 0)


def local(passage_states, query_emb, head_weight, head_bias, norm_gain, candidate_ids):
    owners = lax.axis_size("shard")
    rows, width = passage_states.shape
    queries, cands = candidate_ids.shape
    slab_rows = 8 * 4 * rows
    every = owners * queries
    dma = pltpu.SemaphoreType.DMA
    vmem = pl.BlockSpec(memory_space=pltpu.VMEM)
    hbm = pl.BlockSpec(memory_space=pltpu.HBM)
    loss, grad = pl.pallas_call(
        functools.partial(kernel, owners, rows, queries, cands),
        out_shape=(jax.ShapeDtypeStruct((queries, 128), F32), jax.ShapeDtypeStruct((queries, width), F32)),
        in_specs=[hbm] * 6,
        out_specs=(vmem, vmem),
        scratch_shapes=[
            pltpu.VMEM((rows, width), BF16),
            pltpu.VMEM((queries, width), BF16),
            pltpu.VMEM((width, width), BF16),
            pltpu.VMEM((width,), F32),
            pltpu.VMEM((width,), F32),
            pltpu.VMEM((queries, cands), jnp.int32),
            pltpu.VMEM((2 * queries, width // 2), BF16),
            pltpu.VMEM((8, 128), jnp.int32),
            pltpu.VMEM((slab_rows, width), BF16),
            pltpu.VMEM((2 * every, width // 2), BF16),
            pltpu.VMEM((every, width), BF16),
            pltpu.VMEM((owners * 8, 128), jnp.int32),
            pltpu.VMEM((every, slab_rows), F32),
            pltpu.VMEM((every, slab_rows), F32),
            pltpu.VMEM((every, slab_rows), BF16),
            pltpu.VMEM((every, slab_rows), BF16),
            pltpu.VMEM((4 * every, width // 2), BF16),
            pltpu.VMEM((4 * every, width // 2), BF16),
            pltpu.VMEM((owners, 1, 128), F32),
            pltpu.VMEM((owners, 1, 128), F32),
            dma((6,)),
            dma((16,)), dma((16,)),
            dma((16,)), dma((16,)),
            dma((16,)), dma((16,)),
            dma((32,)), dma((32,)),
            dma((owners,)), dma((owners,)),
            dma((owners,)), dma((owners,)),
            dma((owners,)), dma((owners,)),
            dma((owners,)), dma((owners,)),
        ],
        compiler_params=pltpu.CompilerParams(
            collective_id=0, has_side_effects=True, vmem_limit_bytes=48 * 2**20
        ),
    )(passage_states, query_emb, head_weight, head_bias, norm_gain, candidate_ids)
    return loss[:, 0], grad


def solution(mesh):
    split = P(("group", "shard", "mp"), None)
    in_specs = (split, split, P(), P(), P(), split)
    out_specs = (P(("group", "shard", "mp")), split)
    return jax.shard_map(local, mesh=mesh, in_specs=in_specs, out_specs=out_specs, check_vma=False)
```

time: 187 us -> 106 us (0.57)
  the two profiles are of different devices: /device:TPU:6 before, /device:TPU:933 now
where the time goes in v2:
time: 106 us
  Pallas kernels  99 us (93%)
  local copies, waits for them, and re-layouts  6.15 us (6%)
    pallas_call x1, Pallas kernels, local(): pl.pallas_call(functools.partial(kernel, owners, rows, queries, cands), o...  99 us
    unnamed x13, local copies, waits for them, and re-layouts  5.53 us

profile of v2, /device:TPU:933, one launch (start us, length us, event | category | flops | bytes accessed | tf_op | source)
XLA Modules:
  0.0 105.8 jit_solution(16238522135623961960)
XLA Ops:
  0.6 0.0 copy-start
  0.6 1.3 %copy-done = bf16[768,768]{1,0:T(8,128)(2,1)S(1)} copy-done((bf16[768,768]{1,0:T(8,128)(2,1)S(1)}, bf16[768,768]{1,0:T(8,128)(2,1)}, u32[]{:S(2)}) %copy-start) | copy-done | bytes 1179672
  1.9 0.0 copy-start.1
  1.9 0.9 copy-done.1
  2.8 0.0 copy-start.2
  2.8 0.7 copy-done.2
  3.5 0.0 copy-start.3
  3.5 0.7 copy-done.3
  4.2 0.0 copy-start.4
  4.2 0.7 copy-done.4
  4.9 0.0 copy-start.5
  4.9 0.7 copy-done.5
  5.6 99.0 %shard_map.77 = (f32[8,128]{1,0:T(8,128)S(1)}, f32[8,768]{1,0:T(8,128)S(1)}) custom-call(bf16[64,768]{1,0:T(8,128)(2,1)S(1)} %copy-done.1, bf16[8,768]{1,0:T(8,128)(2,1)S(1)} %copy-done.2, bf16[768,768]{1,0:T(8,128)(2,1)S(1)} %copy-done, f32[768]{0:T(1024)S(1)} %copy-done.3, f32[768]{0:T(1024)S(1)} %copy-done.4, s32[8,65]{1,0:T(8,128)S(1)} %copy-done.5), custom_call_target="tpu_custom_call" | custom-call | tf_op jit(solution)/shard_map/pallas_call | solution.py:396
  104.5 0.6 slice_reduce_fusion
  105.2 0.6 copy.9
Async XLA Ops:
  0.6 1.3 %copy-start = (bf16[768,768]{1,0:T(8,128)(2,1)S(1)}, bf16[768,768]{1,0:T(8,128)(2,1)}, u32[]{:S(2)}) copy-start(bf16[768,768]{1,0:T(8,128)(2,1)} %w_in.1) | copy-start | bytes 3538948
  1.9 0.9 copy-start.1
  2.8 0.7 copy-start.2
  3.5 0.7 copy-start.3
  4.2 0.7 copy-start.4
  4.9 0.7 copy-start.5

commit v3 on v2

--- a/solution.py
+++ b/solution.py
@@ -19,8 +19,8 @@
     states_in, query_in, w_in, bias_in, gain_in, ids_in,
     loss_out, grad_out,
     states, query, w, bias, gain, raw_ids, query_half, ids,
-    slab, qbuf, qmat, idbuf, cnt, score, prob, first, part, parts, stat, stats,
-    load_sems, us, ur, ns, nr, vs, vr, cs, cr, qs, qr, ds, dr, ts, tr, ps, pr,
+    slab, qbuf, qmat, idbuf, cnt, score, both, part, parts, stat, stats,
+    load_sems, us, ur, ns, nr, vs, vr, cs, cr, qs, qr, ds, dr, gs, gr, hs, hr, ts, tr, ps, pr,
 ):
     width = w.shape[0]
     half_width = width // 2
@@ -30,9 +30,11 @@
     two = 2 * queries
     scaling = 1.0 / math.sqrt(width)
     y, s, mp = lax.axis_index("group"), lax.axis_index("shard"), lax.axis_index("mp")
-    x, z = s // 4, lax.rem(s, 4) * 2 + mp // 2
+    x, z_hi = s // 4, lax.rem(s, 4)
+    z = z_hi * 2 + mp // 2
     core, y_lo = lax.rem(mp, 2), lax.rem(y, 2)
-    me = x * 4 + y // 2
+    y_hi = y // 2
+    me = x * 4 + y_hi
     lane = y_lo * 2 + core
     lane_across = lax.rem(lane + 2, 4)
     lane_twin = lane + 1 - 2 * core
@@ -46,7 +48,13 @@
     twin = {"mp": mp + 1 - 2 * core}
 
     def peer(p):
-        return {"group": lax.rem(p, 4) * 2 + y_lo, "shard": p // 4 * 4 + s - x * 4}
+        return {"group": lax.rem(p, 4) * 2 + y_lo, "shard": p // 4 * 4 + z_hi}
+
+    def beside(k):
+        return x * 4 + lax.rem(y_hi + k, 4)
+
+    def column_of(k):
+        return lax.rem(x + k, 8)
 
     def other(k):
         return lax.rem(me + k, owners)
@@ -74,11 +82,10 @@
     greet(across)
     greet(twin)
 
-    def greet_peer(k, carry):
-        greet(peer(other(k)))
-        return carry
-
-    lax.fori_loop(1, owners, greet_peer, 0)
+    for k in range(1, 4):
+        greet(peer(beside(k)))
+    for k in range(1, 8):
+        greet(peer(column_of(k) * 4 + y_hi))
 
     for load in loads:
         load.wait()
@@ -87,7 +94,7 @@
     spread = jnp.mean(centred * centred, axis=-1, keepdims=True)
     normal = centred * lax.rsqrt(spread + 1e-05) * gain[...].reshape(1, width)
     slab[pl.ds(pl.multiple_of(z * span + lane * rows, rows), rows), :] = normal.astype(BF16)
-    pl.semaphore_wait(barrier, owners + 2 + (z > 0).astype(jnp.int32))
+    pl.semaphore_wait(barrier, 13 + (z > 0).astype(jnp.int32))
 
     def send(src, dst, send_sem, recv_sem, device):
         return pltpu.make_async_remote_copy(
@@ -114,10 +121,10 @@
         return send(c, c, cs.at[sem], cr.at[sem], twin)
 
     def reach_up(level):
-        return jnp.where(level >= 6, 3, 7 - level)
+        return jnp.where(level >= 4, 3, 7 - level)
 
     def reach_down(level):
-        return jnp.where(level >= 6, 4, level)
+        return jnp.where(level >= 4, 4, level)
 
     for h in (0, 1):
         up(z, h).start()
@@ -156,32 +163,49 @@
     def d_copy(p, at):
         return send(ids, idbuf.at[d_at(at), :], ds.at[p], dr.at[at], peer(p))
 
-    def share(k, carry):
-        d_copy(other(k), me).start()
-        q_copy(other(k), me).start()
-        return carry
-
-    lax.fori_loop(1, owners, share, 0)
+    def column_copies(column, target):
+        q_four = qbuf.at[pl.ds(pl.multiple_of(column * 4 * two, 4 * two), 4 * two), :]
+        d_four = idbuf.at[pl.ds(pl.multiple_of(column * 32, 32), 32), :]
+        device = peer(target * 4 + y_hi)
+        return (
+            lambda: send(d_four, d_four, gs.at[target], gr.at[column], device),
+            lambda: send(q_four, q_four, hs.at[target], hr.at[column], device),
+        )
+
+    def share():
+        for k in (2, 1, 3):
+            d_copy(beside(k), me).start()
+            q_copy(beside(k), me).start()
+
+    def share_column():
+        for k in range(1, 4):
+            p = beside(k)
+            d_copy(p, p).wait_recv()
+            q_copy(p, p).wait_recv()
+        for which in (0, 1):
+            for k in (4, 3, 5, 2, 6, 1, 7):
+                column_copies(x, column_of(k))[which]().start()
+
+    def await_columns():
+        for k in range(1, 8):
+            for copy in column_copies(column_of(k), column_of(k)):
+                copy().wait_recv()
+
     qbuf[q_at(me), :] = query_half[...]
     idbuf[d_at(me), :] = ids[...]
-
-    def await_share(k, carry):
-        p = other(k)
-        d_copy(p, p).wait_recv()
-        q_copy(p, p).wait_recv()
-        return carry
 
     def multiplicity(j, carry):
         block = idbuf[d_at(j), :]
         sub = lax.broadcasted_iota(jnp.int32, (128, 128), 0)
-        total = jnp.zeros((128, 128), F32)
+        left_hot, right_hot = [], []
         for t in range(queries):
             row = block[t : t + 1, :]
             key = ((row & 0xFFFFF) >> 7) - me * 128
             value = jnp.where((row >> 20) > 0, 129.0, 1.0)
-            left_hot = jnp.where(sub == key, value, 0.0).astype(BF16)
-            right_hot = jnp.where(sub == (row & 127), 1.0, 0.0).astype(BF16)
-            total += lax.dot_general(left_hot, right_hot, NT, preferred_element_type=F32)
+            left_hot.append(jnp.where(sub == key, value, 0.0).astype(BF16))
+            right_hot.append(jnp.where(sub == (row & 127), 1.0, 0.0).astype(BF16))
+        left_hot, right_hot = jnp.concatenate(left_hot, axis=1), jnp.concatenate(right_hot, axis=1)
+        total = lax.dot_general(left_hot, right_hot, NT, preferred_element_type=F32)
         for hi in range(16):
             cnt[d_at(j), hi * 128 : hi * 128 + 128] = total[hi * 8 : hi * 8 + 8, :]
         return carry
@@ -194,15 +218,13 @@
         level = lax.rem(z + k, 8)
         return jnp.logical_and(z + k <= 7, k <= reach_down(level)), level, k + 1 <= reach_down(level), down
 
-    arrivals = []
-    for k in range(1, 8):
-        arrivals.append(rise(k, z >= k))
-        if k <= 5:
-            arrivals.append(fall(k))
-        if k == 3:
-            arrivals.append(rise(z + 1, z <= 2))
-        if k == 4:
-            arrivals.append(rise(z + 2, z <= 1))
+    ups = {k: rise(k, z >= k) for k in range(1, 8)}
+    falls = {k: fall(k) for k in range(1, 5)}
+    wraps = {k: rise(z + k, z + k <= 3) for k in range(1, 4)}
+    arrivals = [
+        ups[1], ups[2], falls[1], ups[3], falls[2], ups[4], falls[3],
+        wraps[1], wraps[2], falls[4], wraps[3], ups[5], ups[6], ups[7],
+    ]
 
     def arrive(event):
         when, level, goes_on, way = event
@@ -236,26 +258,36 @@
         def _():
             do(event[1])
 
-    pass_on(z)
-    for event in arrivals[:4]:
-        arrive(event)
-    for event in arrivals[:3]:
+    arrive(arrivals[0])
+    share()
+
+    def prepare():
+        await_columns()
+        lax.fori_loop(0, owners, multiplicity, 0, unroll=4)
+        halves = qbuf[...].astype(F32).reshape(owners, 2, queries, half_width)
+        qmat[:, :half_width] = halves[:, 0].reshape(every, half_width).astype(BF16)
+        qmat[:, half_width:] = halves[:, 1].reshape(every, half_width).astype(BF16)
+
+    order = [(True, z)] + arrivals
+    met = 9
+    for i in range(2, len(order)):
+        arrive(order[i])
+        later(order[i - 2], pass_on)
+        if i == 3:
+            share_column()
+        if i == met:
+            prepare()
+            for event in order[: met - 3]:
+                later(event, use)
+        if i > met:
+            later(order[i - 4], use)
+    for event in order[-2:]:
         later(event, pass_on)
-    lax.fori_loop(1, owners, await_share, 0)
-    lax.fori_loop(0, owners, multiplicity, 0)
-    halves = qbuf[...].astype(F32).reshape(owners, 2, queries, half_width)
-    qmat[:, :half_width] = halves[:, 0].reshape(every, half_width).astype(BF16)
-    qmat[:, half_width:] = halves[:, 1].reshape(every, half_width).astype(BF16)
-    use(z)
-    later(arrivals[0], use)
-    later(arrivals[1], use)
-    for i in range(4, len(arrivals)):
-        arrive(arrivals[i])
-        later(arrivals[i - 1], pass_on)
-        later(arrivals[i - 2], use)
-    later(arrivals[-1], pass_on)
-    later(arrivals[-2], use)
-    later(arrivals[-1], use)
+    for event in order[-4:]:
+        later(event, use)
+
+    batch = owners // 4
+    per_batch = batch * queries // 16
 
     def softmax(i, carry):
         at = pl.ds(pl.multiple_of(i * 16, 16), 16)
@@ -268,14 +300,15 @@
         e = times * jnp.exp(inside - top)
         total = jnp.sum(e, axis=1, keepdims=True)
         named = jnp.sum(jnp.where(positive, v, 0.0), axis=1, keepdims=True)
-        prob[at, :] = e.astype(BF16)
-        first[at, :] = jnp.where(positive, 1.0, 0.0).astype(BF16)
+        put = pl.multiple_of(i // per_batch * 2 * batch * queries + lax.rem(i, per_batch) * 16, 16)
+        both[pl.ds(put, 16), :] = e.astype(BF16)
+        both[pl.ds(pl.multiple_of(put + batch * queries, 16), 16), :] = jnp.where(positive, 1.0, 0.0).astype(BF16)
         spot = lax.broadcasted_iota(jnp.int32, (16, 128), 1) - 4 * (lax.broadcasted_iota(jnp.int32, (16, 128), 0) & 7)
         tile = jnp.where(spot == 0, top, jnp.where(spot == 1, total, jnp.where(spot == 2, named, 0.0)))
         stat[pl.ds(i * 2, 2), :, :] = jnp.sum(tile.reshape(2, 8, 128), axis=1, keepdims=True)
         return carry
 
-    lax.fori_loop(0, every // 16, softmax, 0)
+    lax.fori_loop(0, every // 16, softmax, 0, unroll=4)
 
     def t_copy(p, at):
         return send(stat.at[p], stats.at[at], ts.at[p], tr.at[at], peer(p))
@@ -293,29 +326,39 @@
     def p_copy(p, frm, at):
         return send(part.at[p_at(frm), :], parts.at[p_at(at), :], ps.at[p], pr.at[at], peer(p))
 
-    batch = owners // 4
-
     def partials(i, carry):
-        b = lax.rem(me // batch + 2 + i, 4)
-        take = pl.ds(pl.multiple_of(b * batch * queries, batch * queries), batch * queries)
-        pieces = []
-        for weights in (prob, first):
-            sums = jnp.dot(weights[take, :], slab[...], preferred_element_type=F32)
-            pieces.append(sums[:, :half_width].reshape(batch, queries, half_width))
-            pieces.append(sums[:, half_width:].reshape(batch, queries, half_width))
+        b = lax.rem(x // 2 + jnp.where(i == 0, 2, jnp.where(i == 1, 1, jnp.where(i == 2, 3, 0))), 4)
+        take = pl.ds(pl.multiple_of(b * 2 * batch * queries, 2 * batch * queries), 2 * batch * queries)
+        sums = jnp.dot(both[take, :], slab[...], preferred_element_type=F32)
+        pieces = [
+            sums[i * batch * queries : (i + 1) * batch * queries, j * half_width : (j + 1) * half_width].reshape(
+                batch, queries, half_width
+            )
+            for i in (0, 1)
+            for j in (0, 1)
+        ]
         put = pl.ds(pl.multiple_of(b * batch * 2 * two, batch * 2 * two), batch * 2 * two)
         part[put, :] = jnp.concatenate(pieces, axis=1).reshape(batch * 2 * two, half_width).astype(BF16)
 
-        def give(k, inner):
-            p = b * batch + lax.rem(me + k, batch)
-
-            @pl.when(p != me)
-            def _():
-                p_copy(p, p, me).start()
-
-            return inner
-
-        lax.fori_loop(0, batch, give, 0)
+        def give(pairs):
+            def one(k, inner):
+                for pair in pairs:
+                    p = lax.rem(x // 2 + pair, 4) * batch + lax.rem(k, 2) * 4 + lax.rem(y_hi + 2 + 3 * (k // 2), 4)
+
+                    @pl.when(p != me)
+                    def _(p=p):
+                        p_copy(p, p, me).start()
+
+                return inner
+
+            lax.fori_loop(0, batch, one, 0)
+
+        for step, pairs in ((0, (2,)), (2, (1, 3)), (3, (0,))):
+
+            @pl.when(i == step)
+            def _(pairs=pairs):
+                give(pairs)
+
         return carry
 
     lax.fori_loop(0, 4, partials, 0)
@@ -354,13 +397,18 @@
 
     def sent(k, carry):
         p = other(k)
-        q_copy(p, me).wait_send()
-        d_copy(p, me).wait_send()
         t_copy(p, me).wait_send()
         p_copy(p, p, me).wait_send()
         return carry
 
     lax.fori_loop(1, owners, sent, 0)
+
+    for k in range(1, 4):
+        d_copy(beside(k), me).wait_send()
+        q_copy(beside(k), me).wait_send()
+    for k in range(1, 8):
+        for copy in column_copies(x, column_of(k)):
+            copy().wait_send()
 
     def sent_rows(level, carry):
         risen, fallen = lax.rem(z - level + 8, 8), level - z
@@ -413,8 +461,7 @@
             pltpu.VMEM((owners * 8, 128), jnp.int32),
             pltpu.VMEM((every, slab_rows), F32),
             pltpu.VMEM((every, slab_rows), F32),
-            pltpu.VMEM((every, slab_rows), BF16),
-            pltpu.VMEM((every, slab_rows), BF16),
+            pltpu.VMEM((2 * every, slab_rows), BF16),
             pltpu.VMEM((4 * every, width // 2), BF16),
             pltpu.VMEM((4 * every, width // 2), BF16),
             pltpu.VMEM((owners, 1, 128), F32),
@@ -426,11 +473,13 @@
             dma((32,)), dma((32,)),
             dma((owners,)), dma((owners,)),
             dma((owners,)), dma((owners,)),
+            dma((8,)), dma((8,)),
+            dma((8,)), dma((8,)),
             dma((owners,)), dma((owners,)),
             dma((owners,)), dma((owners,)),
         ],
         compiler_params=pltpu.CompilerParams(
-            collective_id=0, has_side_effects=True, vmem_limit_bytes=48 * 2**20
+            collective_id=0, has_side_effects=True, vmem_limit_bytes=63 * 2**20
         ),
     )(passage_states, query_emb, head_weight, head_bias, norm_gain, candidate_ids)
     return loss[:, 0], grad

time: 106 us -> 80.7 us (0.76)
  the two profiles are of different devices: /device:TPU:933 before, /device:TPU:1 now
where the time goes in v3:
time: 80.7 us; the launch traced here: 79.3 us
  Pallas kernels  76 us (94%)
  local copies, waits for them, and re-layouts  2.64 us (3%)
    pallas_call x1, Pallas kernels, local(): pl.pallas_call(functools.partial(kernel, owners, rows, queries, cands), o...  76 us

profile of v3, /device:TPU:1, one launch (start us, length us, event | category | flops | bytes accessed | tf_op | source)
XLA Modules:
  0.0 79.3 jit_solution(9031554835298814587)
XLA Ops:
  0.6 76.0 %shard_map.77 = (f32[8,128]{1,0:T(8,128)}, f32[8,768]{1,0:T(8,128)}) custom-call(bf16[64,768]{1,0:T(8,128)(2,1)} %states_in.1, bf16[8,768]{1,0:T(8,128)(2,1)} %query_in.1, bf16[768,768]{1,0:T(8,128)(2,1)} %w_in.1, f32[768]{0:T(1024)} %bias_in.1, f32[768]{0:T(1024)} %gain_in.1, s32[8,65]{1,0:T(8,128)} %ids_in.1), custom_call_target="tpu_custom_call" | custom-call | tf_op jit(solution)/shard_map/pallas_call | solution.py:444
  76.6 1.3 %slice_reduce_fusion = f32[8]{0:T(128)} fusion(f32[8,128]{1,0:T(8,128)} %get-tuple-element.4), kind=kLoop, calls=%fused_computation | loop fusion | bytes 64 | tf_op jit(solution)/shard_map/slice | solution.py:485
  77.9 1.3 %copy.9 = f32[8,768]{1,0:T(8,128)} copy(f32[8,768]{1,0:T(8,128)} %get-tuple-element.9) | data formatting | bytes 49152

commit v4 on v3

--- a/solution.py
+++ b/solution.py
@@ -223,7 +223,7 @@
     wraps = {k: rise(z + k, z + k <= 3) for k in range(1, 4)}
     arrivals = [
         ups[1], ups[2], falls[1], ups[3], falls[2], ups[4], falls[3],
-        wraps[1], wraps[2], falls[4], wraps[3], ups[5], ups[6], ups[7],
+        ups[5], ups[6], ups[7], wraps[1], wraps[2], falls[4], wraps[3],
     ]
 
     def arrive(event):
@@ -261,22 +261,50 @@
     arrive(arrivals[0])
     share()
 
-    def prepare():
-        await_columns()
-        lax.fori_loop(0, owners, multiplicity, 0, unroll=4)
+    def count(step, steps):
+        lax.fori_loop(step * owners // steps, (step + 1) * owners // steps, multiplicity, 0, unroll=4)
+
+    def widen():
         halves = qbuf[...].astype(F32).reshape(owners, 2, queries, half_width)
         qmat[:, :half_width] = halves[:, 0].reshape(every, half_width).astype(BF16)
         qmat[:, half_width:] = halves[:, 1].reshape(every, half_width).astype(BF16)
 
     order = [(True, z)] + arrivals
-    met = 9
+    upper, met = z >= 4, 12
+    lower = jnp.logical_not(upper)
     for i in range(2, len(order)):
         arrive(order[i])
-        later(order[i - 2], pass_on)
+        if i == 9:
+            later((jnp.logical_and(upper, order[7][0]), order[7][1]), pass_on)
+        else:
+            later(order[i - 2], pass_on)
         if i == 3:
             share_column()
+        if 7 <= i <= 10:
+
+            @pl.when(upper)
+            def _(i=i):
+                if i == 7:
+                    await_columns()
+                count(i - 7, 4)
+                if i == 10:
+                    widen()
+
+        if i == 9:
+
+            @pl.when(lower)
+            def _():
+                await_columns()
+                count(0, 2)
+
         if i == met:
-            prepare()
+            later((jnp.logical_and(lower, order[7][0]), order[7][1]), pass_on)
+
+            @pl.when(lower)
+            def _():
+                count(1, 2)
+                widen()
+
             for event in order[: met - 3]:
                 later(event, use)
         if i > met:
@@ -303,8 +331,8 @@
         put = pl.multiple_of(i // per_batch * 2 * batch * queries + lax.rem(i, per_batch) * 16, 16)
         both[pl.ds(put, 16), :] = e.astype(BF16)
         both[pl.ds(pl.multiple_of(put + batch * queries, 16), 16), :] = jnp.where(positive, 1.0, 0.0).astype(BF16)
-        spot = lax.broadcasted_iota(jnp.int32, (16, 128), 1) - 4 * (lax.broadcasted_iota(jnp.int32, (16, 128), 0) & 7)
-        tile = jnp.where(spot == 0, top, jnp.where(spot == 1, total, jnp.where(spot == 2, named, 0.0)))
+        spot = lax.broadcasted_iota(jnp.int32, (16, 128), 1) - (lax.broadcasted_iota(jnp.int32, (16, 128), 0) & 7)
+        tile = jnp.where(spot == 0, top, jnp.where(spot == 8, total, jnp.where(spot == 16, named, 0.0)))
         stat[pl.ds(i * 2, 2), :, :] = jnp.sum(tile.reshape(2, 8, 128), axis=1, keepdims=True)
         return carry
 
@@ -372,9 +400,9 @@
     told_all = stats[...].reshape(owners, 128)
     top = jnp.max(told_all, axis=0, keepdims=True)
     fade = jnp.exp(jnp.minimum(told_all - top, 0.0))
-    total = jnp.sum(pltpu.roll(told_all, 127, 1) * fade, axis=0, keepdims=True)
-    named = jnp.sum(pltpu.roll(told_all, 126, 1), axis=0, keepdims=True)
-    own_spot = lax.broadcasted_iota(jnp.int32, (1, queries, 128), 2) == 4 * lax.broadcasted_iota(
+    total = jnp.sum(pltpu.roll(told_all, 120, 1) * fade, axis=0, keepdims=True)
+    named = jnp.sum(pltpu.roll(told_all, 112, 1), axis=0, keepdims=True)
+    own_spot = lax.broadcasted_iota(jnp.int32, (1, queries, 128), 2) == lax.broadcasted_iota(
         jnp.int32, (1, queries, 128), 1
     )
 
@@ -382,7 +410,7 @@
         return jnp.sum(jnp.where(own_spot, flat.reshape(-1, 1, 128), 0.0), axis=2, keepdims=True)
 
     factor = upright(fade / total)
-    loss_out[...] = jnp.broadcast_to(upright(top + jnp.log(total) - named)[0], (queries, 128))
+    loss_out[...] = jnp.broadcast_to(top + jnp.log(total) - named, (queries, 128))
 
     def taken(k, carry):
         p = other(k)
@@ -430,6 +458,18 @@
         return carry
 
     lax.fori_loop(0, 8, sent_rows, 0)
+
+
+def finish(loss_in, grad_in, loss_out, grad_out, loss, sems):
+    copies = [
+        pltpu.make_async_copy(loss_in, loss, sems.at[0]),
+        pltpu.make_async_copy(grad_in, grad_out, sems.at[1]),
+    ]
+    for copy in copies:
+        copy.start()
+    for copy in copies:
+        copy.wait()
+    loss_out[...] = loss[0, : loss_out.shape[0]]
 
 
 def local(passage_states, query_emb, head_weight, head_bias, norm_gain, candidate_ids):
@@ -482,7 +522,14 @@
             collective_id=0, has_side_effects=True, vmem_limit_bytes=63 * 2**20
         ),
     )(passage_states, query_emb, head_weight, head_bias, norm_gain, candidate_ids)
-    return loss[:, 0], grad
+    return pl.pallas_call(
+        finish,
+        out_shape=(jax.ShapeDtypeStruct((queries,), F32), jax.ShapeDtypeStruct((queries, width), F32)),
+        in_specs=[hbm, hbm],
+        out_specs=(vmem, vmem),
+        scratch_shapes=[pltpu.VMEM((queries, 128), F32), dma((2,))],
+        compiler_params=pltpu.CompilerParams(vmem_limit_bytes=63 * 2**20),
+    )(loss, grad)
 
 
 def solution(mesh):

time: 80.7 us -> 77.3 us (0.958)
  local copies, waits for them, and re-layouts: 2.64 us -> 0 us
    pallas_call x1, Pallas kernels: 76 us -> 74.2 us  [local(): pl.pallas_call(functools.partial(kernel, owners, rows, queries, cands), o...]
    pallas_call x0 -> x1, Pallas kernels: none -> 1.37 us  [local(): pl.pallas_call(finish, out_shape=(jax.ShapeDtypeStruct((queries,), F32),...]
    unnamed x1 -> x0, local copies, waits for them, and re-layouts: 1.35 us -> none
    slice x1 -> x0, local copies, waits for them, and re-layouts: 1.3 us -> none  [local(): return (loss[:, 0], grad)]
where the time goes in v4:
time: 77.3 us; the launch traced here: 76.2 us
  Pallas kernels  75.5 us (98%)
    pallas_call x1, Pallas kernels, local(): pl.pallas_call(functools.partial(kernel, owners, rows, queries, cands), o...  74.2 us

profile of v4, /device:TPU:1, one launch (start us, length us, event | category | flops | bytes accessed | tf_op | source)
XLA Modules:
  0.0 76.2 jit_solution(1297478120307970337)
XLA Ops:
  0.6 74.2 %shard_map.77 = (f32[8,128]{1,0:T(8,128)}, f32[8,768]{1,0:T(8,128)}) custom-call(bf16[64,768]{1,0:T(8,128)(2,1)} %states_in.1, bf16[8,768]{1,0:T(8,128)(2,1)} %query_in.1, bf16[768,768]{1,0:T(8,128)(2,1)} %w_in.1, f32[768]{0:T(1024)} %bias_in.1, f32[768]{0:T(1024)} %gain_in.1, s32[8,65]{1,0:T(8,128)} %ids_in.1), custom_call_target="tpu_custom_call" | custom-call | tf_op jit(solution)/shard_map/pallas_call | solution.py:484
  74.8 1.4 %shard_map.78 = (f32[8]{0:T(128)}, f32[8,768]{1,0:T(8,128)}) custom-call(f32[8,128]{1,0:T(8,128)} %get-tuple-element.4.loss_in, f32[8,768]{1,0:T(8,128)} %get-tuple-element.5.grad_in), custom_call_target="tpu_custom_call" | custom-call | tf_op jit(solution)/shard_map/pallas_call | solution.py:525

commit v5 on v4

--- a/solution.py
+++ b/solution.py
@@ -24,7 +24,7 @@
 ):
     width = w.shape[0]
     half_width = width // 2
-    half = rows // 2
+    half = rows // 1
     span = 4 * rows
     every = owners * queries
     two = 2 * queries
@@ -105,19 +105,19 @@
         return slab.at[pl.ds(pl.multiple_of(level * span + which * rows + h * half, half), half), :]
 
     def up(level, h):
-        c, sem = chunk(level, lane, h), level * 2 + h
+        c, sem = chunk(level, lane, h), level * 1 + h
         return send(c, c, us.at[sem], ur.at[sem], above)
 
     def down(level, h):
-        c, sem = chunk(level, lane, h), level * 2 + h
+        c, sem = chunk(level, lane, h), level * 1 + h
         return send(c, c, ns.at[sem], nr.at[sem], below)
 
     def over(level, h, which):
-        c, sem = chunk(level, which, h), level * 2 + h
+        c, sem = chunk(level, which, h), level * 1 + h
         return send(c, c, vs.at[sem], vr.at[sem], across)
 
     def to_twin(level, h, which):
-        c, sem = chunk(level, which, h), level * 4 + which // 2 * 2 + h
+        c, sem = chunk(level, which, h), level * 2 + which // 2 * 1 + h
         return send(c, c, cs.at[sem], cr.at[sem], twin)
 
     def reach_up(level):
@@ -126,14 +126,14 @@
     def reach_down(level):
         return jnp.where(level >= 4, 4, level)
 
-    for h in (0, 1):
+    for h in range(1):
         up(z, h).start()
 
         @pl.when(z > 0)
         def _(h=h):
             down(z, h).start()
 
-    for h in (0, 1):
+    for h in range(1):
         over(z, h, lane).start()
         to_twin(z, h, lane).start()
 
@@ -231,7 +231,7 @@
 
         @pl.when(when)
         def _():
-            for h in (0, 1):
+            for h in range(1):
                 way(level, h).wait_recv()
 
                 @pl.when(goes_on)
@@ -242,13 +242,13 @@
                 to_twin(level, h, lane).start()
 
     def pass_on(level):
-        for h in (0, 1):
+        for h in range(1):
             over(level, h, lane_across).wait_recv()
             to_twin(level, h, lane_across).start()
 
     def use(level):
         for which in (lane_twin, lane_twin_across):
-            for h in (0, 1):
+            for h in range(1):
                 to_twin(level, h, which).wait_recv()
         at = pl.ds(pl.multiple_of(level * span, span), span)
         score[:, at] = lax.dot_general(qmat[...], slab[at, :], NT, preferred_element_type=F32) * scaling
@@ -345,7 +345,6 @@
         t_copy(other(k), me).start()
         return carry
 
-    lax.fori_loop(1, owners, tell, 0)
     stats[pl.ds(me, 1), :, :] = stat[pl.ds(me, 1), :, :]
 
     def p_at(p):
@@ -381,6 +380,10 @@
 
             lax.fori_loop(0, batch, one, 0)
 
+        @pl.when(i == 1)
+        def _():
+            lax.fori_loop(1, owners, tell, 0)
+
         for step, pairs in ((0, (2,)), (2, (1, 3)), (3, (0,))):
 
             @pl.when(i == step)
@@ -391,6 +394,42 @@
 
     lax.fori_loop(0, 4, partials, 0)
     parts[p_at(me), :] = part[p_at(me), :]
+
+    def sent(k, carry):
+        p = other(k)
+        t_copy(p, me).wait_send()
+        p_copy(p, p, me).wait_send()
+        return carry
+
+    lax.fori_loop(1, owners, sent, 0)
+
+    for k in range(1, 4):
+        d_copy(beside(k), me).wait_send()
+        q_copy(beside(k), me).wait_send()
+    for k in range(1, 8):
+        for copy in column_copies(x, column_of(k)):
+            copy().wait_send()
+
+    def sent_rows(level, carry):
+        risen, fallen = lax.rem(z - level + 8, 8), level - z
+
+        @pl.when(risen + 1 <= reach_up(level))
+        def _():
+            for h in range(1):
+                up(level, h).wait_send()
+
+        @pl.when(jnp.logical_and(fallen >= 0, fallen + 1 <= reach_down(level)))
+        def _():
+            for h in range(1):
+                down(level, h).wait_send()
+
+        for h in range(1):
+            over(level, h, lane).wait_send()
+            to_twin(level, h, lane).wait_send()
+            to_twin(level, h, lane_across).wait_send()
+        return carry
+
+    lax.fori_loop(0, 8, sent_rows, 0)
 
     def told(k, carry):
         t_copy(other(k), other(k)).wait_recv()
@@ -422,42 +461,6 @@
     for i in (0, 1):
         mean_row = jnp.sum(got[:, i] * factor, axis=0)
         grad_out[:, i * half_width : (i + 1) * half_width] = (mean_row - jnp.sum(got[:, 2 + i], axis=0)) * scaling
-
-    def sent(k, carry):
-        p = other(k)
-        t_copy(p, me).wait_send()
-        p_copy(p, p, me).wait_send()
-        return carry
-
-    lax.fori_loop(1, owners, sent, 0)
-
-    for k in range(1, 4):
-        d_copy(beside(k), me).wait_send()
-        q_copy(beside(k), me).wait_send()
-    for k in range(1, 8):
-        for copy in column_copies(x, column_of(k)):
-            copy().wait_send()
-
-    def sent_rows(level, carry):
-        risen, fallen = lax.rem(z - level + 8, 8), level - z
-
-        @pl.when(risen + 1 <= reach_up(level))
-        def _():
-            for h in (0, 1):
-                up(level, h).wait_send()
-
-        @pl.when(jnp.logical_and(fallen >= 0, fallen + 1 <= reach_down(level)))
-        def _():
-            for h in (0, 1):
-                down(level, h).wait_send()
-
-        for h in (0, 1):
-            over(level, h, lane).wait_send()
-            to_twin(level, h, lane).wait_send()
-            to_twin(level, h, lane_across).wait_send()
-        return carry
-
-    lax.fori_loop(0, 8, sent_rows, 0)
 
 
 def finish(loss_in, grad_in, loss_out, grad_out, loss, sems):
@@ -507,10 +510,10 @@
             pltpu.VMEM((owners, 1, 128), F32),
             pltpu.VMEM((owners, 1, 128), F32),
             dma((6,)),
+            dma((8,)), dma((8,)),
+            dma((8,)), dma((8,)),
+            dma((8,)), dma((8,)),
             dma((16,)), dma((16,)),
-            dma((16,)), dma((16,)),
-            dma((16,)), dma((16,)),
-            dma((32,)), dma((32,)),
             dma((owners,)), dma((owners,)),
             dma((owners,)), dma((owners,)),
             dma((8,)), dma((8,)),

time: 77.3 us -> 75.3 us (0.974); the launches traced: 76.2 us -> 75.1 us
  Pallas kernels: 75.5 us -> 74.4 us
    pallas_call x1, Pallas kernels: 74.2 us -> 73.1 us  [local(): pl.pallas_call(functools.partial(kernel, owners, rows, queries, cands), o...]
where the time goes in v5:
time: 75.3 us; the launch traced here: 75.1 us
  Pallas kernels  74.4 us (99%)
    pallas_call x1, Pallas kernels, local(): pl.pallas_call(functools.partial(kernel, owners, rows, queries, cands), o...  73.1 us

profile of v5, /device:TPU:1, one launch (start us, length us, event | category | flops | bytes accessed | tf_op | source)
XLA Modules:
  0.0 75.1 jit_solution(1630464475143983430)
XLA Ops:
  0.6 73.1 %shard_map.77 = (f32[8,128]{1,0:T(8,128)}, f32[8,768]{1,0:T(8,128)}) custom-call(bf16[64,768]{1,0:T(8,128)(2,1)} %states_in.1, bf16[8,768]{1,0:T(8,128)(2,1)} %query_in.1, bf16[768,768]{1,0:T(8,128)(2,1)} %w_in.1, f32[768]{0:T(1024)} %bias_in.1, f32[768]{0:T(1024)} %gain_in.1, s32[8,65]{1,0:T(8,128)} %ids_in.1), custom_call_target="tpu_custom_call" | custom-call | tf_op jit(solution)/shard_map/pallas_call | solution.py:487
  73.7 1.4 %shard_map.78 = (f32[8]{0:T(128)}, f32[8,768]{1,0:T(8,128)}) custom-call(f32[8,128]{1,0:T(8,128)} %get-tuple-element.4.loss_in, f32[8,768]{1,0:T(8,128)} %get-tuple-element.5.grad_in), custom_call_target="tpu_custom_call" | custom-call | tf_op jit(solution)/shard_map/pallas_call | solution.py:528

commit v6 on v5

--- a/solution.py
+++ b/solution.py
@@ -336,17 +336,10 @@
         stat[pl.ds(i * 2, 2), :, :] = jnp.sum(tile.reshape(2, 8, 128), axis=1, keepdims=True)
         return carry
 
-    lax.fori_loop(0, every // 16, softmax, 0, unroll=4)
 
     def t_copy(p, at):
         return send(stat.at[p], stats.at[at], ts.at[p], tr.at[at], peer(p))
 
-    def tell(k, carry):
-        t_copy(other(k), me).start()
-        return carry
-
-    stats[pl.ds(me, 1), :, :] = stat[pl.ds(me, 1), :, :]
-
     def p_at(p):
         return pl.ds(pl.multiple_of(p * 2 * two, 2 * two), 2 * two)
 
@@ -355,6 +348,7 @@
 
     def partials(i, carry):
         b = lax.rem(x // 2 + jnp.where(i == 0, 2, jnp.where(i == 1, 1, jnp.where(i == 2, 3, 0))), 4)
+        lax.fori_loop(0, per_batch, lambda t, c: softmax(b * per_batch + t, c), 0, unroll=4)
         take = pl.ds(pl.multiple_of(b * 2 * batch * queries, 2 * batch * queries), 2 * batch * queries)
         sums = jnp.dot(both[take, :], slab[...], preferred_element_type=F32)
         pieces = [
@@ -375,14 +369,11 @@
                     @pl.when(p != me)
                     def _(p=p):
                         p_copy(p, p, me).start()
+                        t_copy(p, me).start()
 
                 return inner
 
             lax.fori_loop(0, batch, one, 0)
-
-        @pl.when(i == 1)
-        def _():
-            lax.fori_loop(1, owners, tell, 0)
 
         for step, pairs in ((0, (2,)), (2, (1, 3)), (3, (0,))):
 
@@ -394,6 +385,7 @@
 
     lax.fori_loop(0, 4, partials, 0)
     parts[p_at(me), :] = part[p_at(me), :]
+    stats[pl.ds(me, 1), :, :] = stat[pl.ds(me, 1), :, :]
 
     def sent(k, carry):
         p = other(k)

time: 75.3 us -> 75 us (level)
  no operation moved by 1% of the time
where the time goes in v6:
time: 75 us; the launch traced here: 74.4 us
  Pallas kernels  73.8 us (98%)
    pallas_call x1, Pallas kernels, local(): pl.pallas_call(functools.partial(kernel, owners, rows, queries, cands), o...  72.4 us

profile of v6, /device:TPU:1, one launch (start us, length us, event | category | flops | bytes accessed | tf_op | source)
XLA Modules:
  0.0 74.4 jit_solution(3999338203970305511)
XLA Ops:
  0.6 72.4 %shard_map.77 = (f32[8,128]{1,0:T(8,128)}, f32[8,768]{1,0:T(8,128)}) custom-call(bf16[64,768]{1,0:T(8,128)(2,1)} %states_in.1, bf16[8,768]{1,0:T(8,128)(2,1)} %query_in.1, bf16[768,768]{1,0:T(8,128)(2,1)} %w_in.1, f32[768]{0:T(1024)} %bias_in.1, f32[768]{0:T(1024)} %gain_in.1, s32[8,65]{1,0:T(8,128)} %ids_in.1), custom_call_target="tpu_custom_call" | custom-call | tf_op jit(solution)/shard_map/pallas_call | solution.py:479
  73.1 1.4 %shard_map.78 = (f32[8]{0:T(128)}, f32[8,768]{1,0:T(8,128)}) custom-call(f32[8,128]{1,0:T(8,128)} %get-tuple-element.4.loss_in, f32[8,768]{1,0:T(8,128)} %get-tuple-element.5.grad_in), custom_call_target="tpu_custom_call" | custom-call | tf_op jit(solution)/shard_map/pallas_call | solution.py:520
